TPU v7x, 32 devices: a whole 2x2x4 slice. The times are simulated.
32 devices in a mesh: rows: 4 (over y, x), cols: 8 (over z, core).
Axes of the slice: x: 2, y: 2, z: 4, core: 2. Of those that a mesh axis runs over, the one named last changes fastest.
Arguments:
- c_eta: float32 [512, 2048], P('rows', 'cols'), may hold values from -4 to 4
- c_flux: float32 [2, 512, 2048], P(None, 'rows', 'cols'), may hold values from -150 to 150
- c_depth: float32 [512, 2048], P('rows', 'cols'), may hold values from 100 to 4000
- f_bed: float32 [128, 2048], P('rows', 'cols'), may hold values from -3 to 1
- f_depth: float32 [128, 2048], P('rows', 'cols'), may hold values from 0.05 to 3
- f_wet: int32 [128, 2048], P('rows', 'cols'), may hold values 0 or 1
- f_class: int32 [128, 2048], P('rows', 'cols'), may hold values from 0 to 10
- manning: float32 [11], replicated, may hold values from 0.02 to 0.2
- nest_map: int32 [2048], replicated, may hold values from 0 to 1048575, as said below
Outputs:
- c_eta_out: float32 [512, 2048], P('rows', 'cols')
- f_water: float32 [128, 2048], P('rows', 'cols')
- f_flux: float32 [2, 128, 2048], P(None, 'rows', 'cols')
Inputs may be any that keep to these rules, and one draw needn't show every extreme that they name: `nest_map`: entry b is the flat index, row times 2048 plus column, of the coarse cell that drives fine boundary cell b; entries with the same b // 18 are equal; for s = b // 18 the coarse row lies in [(s * 128) % 512, (s * 128) % 512 + 128) and the coarse column is min(s * 18 * 1 + 256 + j, 2047) for some j in 0..128.
All inputs are finite; a program needn't handle non-finite values. No bound on the sum of `f_wet` on one device may be relied on, other than what follows from the above.
Results may differ from a plain program's by a relative error of at most 0.00002.
Values sent between devices are 32-bit elements; how exact they have to be, the bound alone decides.
A program may use at most 64 MiB of HBM per device.

v0:
```python
import jax
import jax.numpy as jnp
from jax import lax
from jax.sharding import PartitionSpec as P

NCLASS = 11
CSTEPS = 2
SUB = 3
FSTEPS = 6
gravity = 9.81
coarse_spacing = 90.0
coarse_tick = 0.25
fine_spacing = 5.0
depth_floor = 0.01
dry_depth = 0.05


def padded_2(block, sides, width):
    for axis, dim in sides:
        count = lax.axis_size(axis)
        forward = [(i, i + 1) for i in range(count - 1)]
        backward = [(target, source) for source, target in forward]
        low = lax.ppermute(
            lax.slice_in_dim(block, block.shape[dim] - width, None, axis=dim), axis, forward
        )
        high = lax.ppermute(lax.slice_in_dim(block, 0, width, axis=dim), axis, backward)
        block = jnp.concatenate([low, block, high], axis=dim)
    return block


def coarse_update(padded):
    surf = padded[0]
    total = padded[1]
    rows_flux = padded[2]
    cols_flux = padded[3]
    face_rows = jnp.minimum(total[:-1, 1:-1], total[1:, 1:-1])
    new_rows = jnp.minimum(face_rows, 1.0) * (
        rows_flux[:-1, 1:-1]
        - coarse_tick * gravity * face_rows * (surf[1:, 1:-1] - surf[:-1, 1:-1]) / coarse_spacing
    )
    face_cols = jnp.minimum(total[1:-1, :-1], total[1:-1, 1:])
    new_cols = jnp.minimum(face_cols, 1.0) * (
        cols_flux[1:-1, :-1]
        - coarse_tick * gravity * face_cols * (surf[1:-1, 1:] - surf[1:-1, :-1]) / coarse_spacing
    )
    surface = surf[1:-1, 1:-1] - coarse_tick / coarse_spacing * (
        new_rows[1:] - new_rows[:-1] + (new_cols[:, 1:] - new_cols[:, :-1])
    )
    return (surface, new_rows[1:], new_cols[:, 1:])


def face_flux(flux_old, face_depth, slope, rough, fine_tick):
    wetness = jnp.minimum(face_depth / dry_depth, 1.0)
    driven = flux_old - fine_tick * gravity * face_depth * slope / fine_spacing
    friction = 1.0 + fine_tick * gravity * rough * rough * jnp.abs(flux_old) / jnp.power(
        jnp.maximum(face_depth, depth_floor), 7.0 / 3.0
    )
    return wetness * driven / friction


def fine_faces(water_pad, bed_pad, rough_pad, rows_pad, cols_pad, fine_tick):
    surf = bed_pad + water_pad
    depth_rows = jnp.maximum(
        jnp.maximum(surf[:-1, 1:-1], surf[1:, 1:-1])
        - jnp.maximum(bed_pad[:-1, 1:-1], bed_pad[1:, 1:-1]),
        0.0,
    )
    rough_rows = 0.5 * (rough_pad[:-1, 1:-1] + rough_pad[1:, 1:-1])
    new_rows = face_flux(
        rows_pad[:-1, 1:-1], depth_rows, surf[1:, 1:-1] - surf[:-1, 1:-1], rough_rows, fine_tick
    )
    depth_cols = jnp.maximum(
        jnp.maximum(surf[1:-1, :-1], surf[1:-1, 1:])
        - jnp.maximum(bed_pad[1:-1, :-1], bed_pad[1:-1, 1:]),
        0.0,
    )
    rough_cols = 0.5 * (rough_pad[1:-1, :-1] + rough_pad[1:-1, 1:])
    new_cols = face_flux(
        cols_pad[1:-1, :-1], depth_cols, surf[1:-1, 1:] - surf[1:-1, :-1], rough_cols, fine_tick
    )
    return (new_rows, new_cols)


def open_boundary(water_top, bed_top, bnd_surface, bnd_velocity):
    return water_top * bnd_velocity + jnp.sqrt(gravity * jnp.maximum(water_top, depth_floor)) * (
        bnd_surface - (bed_top + water_top)
    )


def blend(levels_stack, fine_index):
    lower = fine_index // SUB
    weight = (fine_index % SUB + 1) / SUB
    return (1.0 - weight) * levels_stack[lower] + weight * levels_stack[lower + 1]


def per_device(c_eta, c_flux, c_depth, f_bed, f_depth, f_wet, f_class, manning, nest_map):
    row_index = lax.axis_index("rows")
    col_index = lax.axis_index("cols")
    row_count = lax.axis_size("rows")
    col_count = lax.axis_size("cols")
    tile_rows, tile_cols = c_eta.shape
    fine_rows_dev, fine_cols_dev = f_bed.shape
    coarse_width = tile_cols * col_count
    coarse_row = nest_map // coarse_width
    coarse_col = nest_map % coarse_width
    local_row = coarse_row - row_index * tile_rows
    local_col = coarse_col - col_index * tile_cols
    owned = (local_row >= 0) & (local_row < tile_rows) & (local_col >= 0) & (local_col < tile_cols)
    flat_index = jnp.where(owned, local_row * tile_cols + local_col, 0)
    owned_weight = jnp.where(owned, 1.0, 0.0)

    def sample(surface, rows_flux):
        velocity = rows_flux / (c_depth + surface)
        return jnp.stack(
            [
                jnp.take(surface.reshape(-1), flat_index) * owned_weight,
                jnp.take(velocity.reshape(-1), flat_index) * owned_weight,
            ]
        )

    surface = c_eta
    rows_flux = c_flux[0]
    cols_flux = c_flux[1]
    sampled = [sample(surface, rows_flux)]
    for coarse_index in range(CSTEPS):
        stacked = jnp.stack([surface, c_depth + surface, rows_flux, cols_flux])
        padded = padded_2(stacked, (("rows", 1), ("cols", 2)), 1)
        surface, rows_flux, cols_flux = coarse_update(padded)
        sampled.append(sample(surface, rows_flux))
    levels_stack = jnp.stack(sampled)
    per_step = jnp.stack([blend(levels_stack, fine_index) for fine_index in range(FSTEPS)])
    summed = lax.psum(per_step, ("rows", "cols"))
    boundary = lax.dynamic_slice_in_dim(summed, col_index * fine_cols_dev, fine_cols_dev, 2)
    roughness = jnp.zeros_like(f_bed)
    for class_index in range(NCLASS):
        roughness = jnp.where(f_class == class_index, manning[class_index], roughness)
    water = f_wet.astype(f_bed.dtype) * f_depth
    fine_rows = jnp.zeros_like(water)
    fine_cols = jnp.zeros_like(water)
    fine_tick = coarse_tick / SUB
    row_start = row_index * fine_rows_dev
    col_start = col_index * fine_cols_dev
    total_rows = fine_rows_dev * row_count
    total_cols = fine_cols_dev * col_count
    col_faces = col_start + jnp.arange(fine_cols_dev + 1)
    col_keep = jnp.where((col_faces == 0) | (col_faces == total_cols), 0.0, 1.0)[None, :]
    static_pad = padded_2(jnp.stack([f_bed, roughness]), (("rows", 1), ("cols", 2)), 1)
    bed_pad = static_pad[0]
    rough_pad = static_pad[1]
    row_faces = row_start + jnp.arange(fine_rows_dev + 1)
    row_keep = jnp.where(row_faces == total_rows, 0.0, 1.0)[:, None]
    at_top = row_index == 0
    for fine_index in range(FSTEPS):
        state_pad = padded_2(
            jnp.stack([water, fine_rows, fine_cols]), (("rows", 1), ("cols", 2)), 1
        )
        water_pad = state_pad[0]
        new_rows, new_cols = fine_faces(
            water_pad, bed_pad, rough_pad, state_pad[1], state_pad[2], fine_tick
        )
        new_rows = new_rows * row_keep
        new_cols = new_cols * col_keep
        top_flux = open_boundary(
            water_pad[1, 1:-1], bed_pad[1, 1:-1], boundary[fine_index, 0], boundary[fine_index, 1]
        )
        first_face = jnp.where(at_top, top_flux, new_rows[0])
        new_rows = jnp.concatenate([first_face[None, :], new_rows[1:]], axis=0)
        water = water_pad[1:-1, 1:-1] - fine_tick / fine_spacing * (
            new_rows[1:] - new_rows[:-1] + (new_cols[:, 1:] - new_cols[:, :-1])
        )
        fine_rows = new_rows[1:]
        fine_cols = new_cols[:, 1:]
    return (surface, water, jnp.stack([fine_rows, fine_cols]))


def solution(mesh):
    in_specs = (
        P("rows", "cols"),
        P(None, "rows", "cols"),
        P("rows", "cols"),
        P("rows", "cols"),
        P("rows", "cols"),
        P("rows", "cols"),
        P("rows", "cols"),
        P(),
        P(),
    )
    out_specs = (P("rows", "cols"), P("rows", "cols"), P(None, "rows", "cols"))
    return jax.shard_map(
        per_device, mesh=mesh, in_specs=in_specs, out_specs=out_specs, check_vma=False
    )
```

profile of v0, /device:TPU:1, one launch (start us, length us, event | category | flops | bytes accessed | tf_op | source)
XLA Modules:
  0.0 376.3 jit_solution(18096316524865931316)
XLA Ops:
  7.2 1.1 fusion.22
  8.4 3.9 %collective-permute-start = (f32[4,1,256]{2,1,0:T(1,128)S(1)}, f32[4,1,256]{2,1,0:T(1,128)S(1)}, u32[]{:S(2)}, u32[]{:S(2)}) collective-permute-start(f32[4,1,256]{2,1,0:T(1,128)S(1)} %get-tuple-element.32), channel_id=1, source_target_pairs={{0,8},{8,16},{16,24},{1,9},{9,17},{17,25},{2,10},{10,18},{18,26},{... | collective-permute-start | bytes 12296 | tf_op jit(solution)/shard_map/ppermute | solution.py:23
  12.4 1.3 collective-permute-start.1
  14.4 7.0 %select_bitcast_fusion = f32[1,32,256]{2,1,0:T(8,128)S(1)} fusion(s32[32,256]{1,0:T(8,128)S(1)} %copy-done.9, f32[]{:T(128)} %bitcast.27, f32[]{:T(128)} %bitcast.26, f32[]{:T(128)} %bitcast.25, f32[]{:T(128)} %bitcast.24, f32[]{:T(128)} %bitcast.23, f32[]{:T(128)} %bitcast.22, f32[]{:T(128)} %bitcast.21, f32[]{:T(128)} %bitcast.20, f32[]{:T(128)} %bitcast.19, ...), kind=kLoop, calls=%fused_computation.156 | loop fusion | flops 180224 | bytes 65580 | tf_op jit(solution)/shard_map/stack | solution.py:147
  21.4 4.0 %collective-permute-start.12 = (f32[2,1,256]{2,1,0:T(1,128)S(1)}, f32[2,1,256]{2,1,0:T(1,128)S(1)}, u32[]{:S(2)}, u32[]{:S(2)}) collective-permute-start(f32[2,1,256]{2,1,0:T(1,128)S(1)} %get-tuple-element.82), channel_id=1, source_target_pairs={{0,8},{8,16},{16,24},{1,9},{9,17},{17,25},{2,10},{10,18},{18,26},{... | collective-permute-start | bytes 6152 | tf_op jit(solution)/shard_map/ppermute | solution.py:23
  25.4 1.3 collective-permute-start.13
  26.8 4.7 %collective-permute-start.8 = (f32[3,1,256]{2,1,0:T(1,128)S(1)}, f32[3,1,256]{2,1,0:T(1,128)S(1)}, u32[]{:S(2)}, u32[]{:S(2)}) collective-permute-start(f32[3,1,256]{2,1,0:T(1,128)S(1)} %get-tuple-element.108), channel_id=1, source_target_pairs={{0,8},{8,16},{16,24},{1,9},{9,17},{17,25},{2,10},{10,18},{18,26},{... | collective-permute-start | bytes 9224 | tf_op jit(solution)/shard_map/ppermute | solution.py:23
  32.3 11.8 %gather_fusion.1 = f32[2048]{0:T(1024)S(1)} fusion(f32[32768]{0:T(1024)S(1)} %bitcast.271, s32[2048]{0:T(1024)S(1)} %get-tuple-element.10), kind=kCustom, calls=%fused_computation.1.clone | custom fusion | bytes 24576 | tf_op jit(solution)/shard_map/jit(_take)/gather | solution.py:117
  44.1 11.8 %gather_fusion = f32[2048]{0:T(1024)S(1)} fusion(f32[32768]{0:T(1024)S(1)} %bitcast.272, s32[2048]{0:T(1024)S(1)} %get-tuple-element.10), kind=kCustom, calls=%fused_computation.clone | custom fusion | bytes 24576 | tf_op jit(solution)/shard_map/jit(_take)/gather | solution.py:116
  56.0 4.9 %collective-permute-start.14 = (f32[2,34,1]{2,1,0:T(8,128)S(1)}, f32[2,34,1]{2,1,0:T(8,128)S(1)}, u32[]{:S(2)}, u32[]{:S(2)}) collective-permute-start(f32[2,34,1]{2,1,0:T(8,128)S(1)} %get-tuple-element.80), channel_id=1, source_target_pairs={{0,1},{1,2},{2,3},{3,4},{4,5},{5,6},{6,7},{8,9},{9,10},{10,11},{11... | collective-permute-start | bytes 824 | tf_op jit(solution)/shard_map/ppermute | solution.py:23
  60.9 1.9 collective-permute-start.15
  62.9 1.3 collective-permute-start.9
  64.2 2.3 collective-permute-done.15
  66.6 1.8 collective-permute-done.9
  68.5 4.5 %collective-permute-start.10 = (f32[3,34,1]{2,1,0:T(8,128)S(1)}, f32[3,34,1]{2,1,0:T(8,128)S(1)}, u32[]{:S(2)}, u32[]{:S(2)}) collective-permute-start(f32[3,34,1]{2,1,0:T(8,128)S(1)} %get-tuple-element.68), channel_id=1, source_target_pairs={{0,1},{1,2},{2,3},{3,4},{4,5},{5,6},{6,7},{8,9},{9,10},{10,11},{11... | collective-permute-start | bytes 1232 | tf_op jit(solution)/shard_map/ppermute | solution.py:23
  73.0 1.9 collective-permute-start.11
  75.0 3.6 collective-permute-done.11
  78.9 1.9 collective-permute-start.2
  80.9 2.4 collective-permute-start.3
  83.3 1.0 collective-permute-done.2
  84.3 4.4 %collective-permute-done.3 = f32[4,130,1]{2,1,0:T(8,128)S(1)} collective-permute-done((f32[4,130,1]{2,1,0:T(8,128)S(1)}, f32[4,130,1]{2,1,0:T(8,128)S(1)}, u32[]{:S(2)}, u32[]{:S(2)}) %collective-permute-start.3) | collective-permute-done | bytes 2112 | tf_op jit(solution)/shard_map/ppermute | solution.py:26
  90.5 4.5 %collective-permute-start.4 = (f32[4,1,256]{2,1,0:T(1,128)S(1)}, f32[4,1,256]{2,1,0:T(1,128)S(1)}, u32[]{:S(2)}, u32[]{:S(2)}) collective-permute-start(f32[4,1,256]{2,1,0:T(1,128)S(1)} %get-tuple-element.30), channel_id=1, source_target_pairs={{0,8},{8,16},{16,24},{1,9},{9,17},{17,25},{2,10},{10,18},{18,26},{... | collective-permute-start | bytes 12296 | tf_op jit(solution)/shard_map/ppermute | solution.py:23
  95.1 1.3 collective-permute-start.5
  96.5 2.9 collective-permute-done.5
  99.6 3.2 collective-permute-start.6
  102.8 1.9 collective-permute-start.7
  105.0 11.8 %gather_fusion.2 = f32[2048]{0:T(1024)S(1)} fusion(f32[32768]{0:T(1024)S(1)} %bitcast.275, s32[2048]{0:T(1024)S(1)} %get-tuple-element.10), kind=kCustom, calls=%fused_computation.2.clone | custom fusion | bytes 24576 | tf_op jit(solution)/shard_map/jit(_take)/gather | solution.py:116
  116.8 11.8 %gather_fusion.3 = f32[2048]{0:T(1024)S(1)} fusion(f32[32768]{0:T(1024)S(1)} %bitcast.274, s32[2048]{0:T(1024)S(1)} %get-tuple-element.10), kind=kCustom, calls=%fused_computation.3.clone | custom fusion | bytes 24576 | tf_op jit(solution)/shard_map/jit(_take)/gather | solution.py:117
  130.4 11.8 %gather_fusion.4 = f32[2048]{0:T(1024)S(1)} fusion(f32[32768]{0:T(1024)S(1)} %bitcast.276, s32[2048]{0:T(1024)S(1)} %get-tuple-element.10), kind=kCustom, calls=%fused_computation.4.clone | custom fusion | bytes 24576 | tf_op jit(solution)/shard_map/jit(_take)/gather | solution.py:116
  142.2 11.8 %gather_fusion.5 = f32[2048]{0:T(1024)S(1)} fusion(f32[32768]{0:T(1024)S(1)} %bitcast.273, s32[2048]{0:T(1024)S(1)} %get-tuple-element.10), kind=kCustom, calls=%fused_computation.5.clone | custom fusion | bytes 24576 | tf_op jit(solution)/shard_map/jit(_take)/gather | solution.py:117
  155.0 120.0 %all-reduce.3.cloned.1.call-done = f32[6,2,2048]{2,1,0:T(2,128)} async-done(((f32[6,2,2048]{2,1,0:T(2,128)}), f32[6,2,2048]{2,1,0:T(2,128)}) %all-reduce.3.cloned.1.call-update) | async-done | bytes 98320 | tf_op jit(solution)/shard_map/psum | solution.py:132
  276.0 3.1 collective-permute-start.16
  279.1 1.3 collective-permute-start.17
  280.4 3.0 collective-permute-done.17
  283.5 7.1 %collective-permute-start.18 = (f32[3,34,1]{2,1,0:T(8,128)S(1)}, f32[3,34,1]{2,1,0:T(8,128)S(1)}, u32[]{:S(2)}, u32[]{:S(2)}) collective-permute-start(f32[3,34,1]{2,1,0:T(8,128)S(1)} %get-tuple-element.64), channel_id=1, source_target_pairs={{0,1},{1,2},{2,3},{3,4},{4,5},{5,6},{6,7},{8,9},{9,10},{10,11},{11... | collective-permute-start | bytes 1232 | tf_op jit(solution)/shard_map/ppermute | solution.py:23
  290.7 1.9 collective-permute-start.19
  292.6 3.6 collective-permute-done.19
  296.7 0.9 broadcast_select_fusion.4
  297.7 4.0 %collective-permute-start.20 = (f32[3,1,256]{2,1,0:T(1,128)S(1)}, f32[3,1,256]{2,1,0:T(1,128)S(1)}, u32[]{:S(2)}, u32[]{:S(2)}) collective-permute-start(f32[3,1,256]{2,1,0:T(1,128)S(1)} %get-tuple-element.76), channel_id=1, source_target_pairs={{0,8},{8,16},{16,24},{1,9},{9,17},{17,25},{2,10},{10,18},{18,26},{... | collective-permute-start | bytes 9224 | tf_op jit(solution)/shard_map/ppermute | solution.py:23
  301.7 1.3 collective-permute-start.21
  303.0 3.0 collective-permute-done.21
  306.1 3.3 collective-permute-start.22
  309.4 1.9 collective-permute-start.23
  311.4 3.6 collective-permute-done.23
  315.5 0.8 broadcast_select_fusion.3
  316.4 2.5 collective-permute-start.24
  319.0 1.3 collective-permute-start.25
  320.3 3.0 collective-permute-done.25
  323.4 3.3 collective-permute-start.26
  326.7 1.9 collective-permute-start.27
  328.6 3.6 collective-permute-done.27
  332.7 0.8 broadcast_select_fusion.2
  333.7 2.5 collective-permute-start.28
  336.2 1.3 collective-permute-start.29
  337.6 3.0 collective-permute-done.29
  340.7 3.3 collective-permute-start.30
  344.0 1.9 collective-permute-start.31
  345.9 3.6 collective-permute-done.31
  351.0 2.5 collective-permute-start.32
  353.5 1.3 collective-permute-start.33
  354.8 3.0 collective-permute-done.33
  357.9 3.3 collective-permute-start.34
  361.3 1.9 collective-permute-start.35
  363.2 3.6 collective-permute-done.35
  (150 shorter events, 14.6 us)
Async XLA Ops:
  7.2 1.2 copy-start
  7.2 1.2 copy-start.1
  7.2 267.9 %all-reduce.3.cloned.1.call-start = ((), (), s32[]{:S(2)}) async-start(), calls=%async_computation | async-start | bytes 196608 | tf_op jit(solution)/shard_map/psum | solution.py:132
  8.4 5.3 %copy-start.6 = (f32[11]{0:T(128)S(1)}, f32[11]{0:T(128)}, u32[]{:S(2)}) copy-start(f32[11]{0:T(128)} %param.18) | copy-start | bytes 136
  8.4 6.0 %copy-start.9 = (s32[32,256]{1,0:T(8,128)S(1)}, s32[32,256]{1,0:T(8,128)}, u32[]{:S(2)}) copy-start(s32[32,256]{1,0:T(8,128)} %param.17) | copy-start | bytes 98308
  8.4 70.3 %collective-permute-start = (f32[4,1,256]{2,1,0:T(1,128)S(1)}, f32[4,1,256]{2,1,0:T(1,128)S(1)}, u32[]{:S(2)}, u32[]{:S(2)}) collective-permute-start(f32[4,1,256]{2,1,0:T(1,128)S(1)} %get-tuple-element.32), channel_id=1, source_target_pairs={{0,8},{8,16},{16,24},{1,9},{9,17},{17,25},{2,10},{10,18},{18,26},{... | collective-permute-start | bytes 12296 | tf_op jit(solution)/shard_map/ppermute | solution.py:23
  12.4 66.4 %collective-permute-start.1 = (f32[4,1,256]{2,1,0:T(1,128)S(1)}, f32[4,1,256]{2,1,0:T(1,128)S(1)}, u32[]{:S(2)}, u32[]{:S(2)}) collective-permute-start(f32[4,1,256]{2,1,0:T(1,128)S(1)} %get-tuple-element.33), channel_id=1, source_target_pairs={{8,0},{16,8},{24,16},{9,1},{17,9},{25,17},{10,2},{18,10},{26,18},{... | collective-permute-start | bytes 12296 | tf_op jit(solution)/shard_map/ppermute | solution.py:26
  14.4 7.0 %copy-start.4 = (f32[32,256]{1,0:T(8,128)S(1)}, f32[32,256]{1,0:T(8,128)}, u32[]{:S(2)}) copy-start(f32[32,256]{1,0:T(8,128)} %param.14) | copy-start | bytes 98308
  21.4 5.3 %copy-start.7 = (f32[32,256]{1,0:T(8,128)S(1)}, f32[32,256]{1,0:T(8,128)}, u32[]{:S(2)}) copy-start(f32[32,256]{1,0:T(8,128)} %param.15) | copy-start | bytes 98308
  21.4 5.3 %copy-start.8 = (s32[32,256]{1,0:T(8,128)S(1)}, s32[32,256]{1,0:T(8,128)}, u32[]{:S(2)}) copy-start(s32[32,256]{1,0:T(8,128)} %param.16) | copy-start | bytes 98308
  21.4 34.5 %collective-permute-start.12 = (f32[2,1,256]{2,1,0:T(1,128)S(1)}, f32[2,1,256]{2,1,0:T(1,128)S(1)}, u32[]{:S(2)}, u32[]{:S(2)}) collective-permute-start(f32[2,1,256]{2,1,0:T(1,128)S(1)} %get-tuple-element.82), channel_id=1, source_target_pairs={{0,8},{8,16},{16,24},{1,9},{9,17},{17,25},{2,10},{10,18},{18,26},{... | collective-permute-start | bytes 6152 | tf_op jit(solution)/shard_map/ppermute | solution.py:23
  25.4 30.5 %collective-permute-start.13 = (f32[2,1,256]{2,1,0:T(1,128)S(1)}, f32[2,1,256]{2,1,0:T(1,128)S(1)}, u32[]{:S(2)}, u32[]{:S(2)}) collective-permute-start(f32[2,1,256]{2,1,0:T(1,128)S(1)} %get-tuple-element.83), channel_id=1, source_target_pairs={{8,0},{16,8},{24,16},{9,1},{17,9},{25,17},{10,2},{18,10},{26,18},{... | collective-permute-start | bytes 6152 | tf_op jit(solution)/shard_map/ppermute | solution.py:26
  26.8 39.8 %collective-permute-start.8 = (f32[3,1,256]{2,1,0:T(1,128)S(1)}, f32[3,1,256]{2,1,0:T(1,128)S(1)}, u32[]{:S(2)}, u32[]{:S(2)}) collective-permute-start(f32[3,1,256]{2,1,0:T(1,128)S(1)} %get-tuple-element.108), channel_id=1, source_target_pairs={{0,8},{8,16},{16,24},{1,9},{9,17},{17,25},{2,10},{10,18},{18,26},{... | collective-permute-start | bytes 9224 | tf_op jit(solution)/shard_map/ppermute | solution.py:23
  31.4 0.7 copy-start.10
  56.0 6.8 %collective-permute-start.14 = (f32[2,34,1]{2,1,0:T(8,128)S(1)}, f32[2,34,1]{2,1,0:T(8,128)S(1)}, u32[]{:S(2)}, u32[]{:S(2)}) collective-permute-start(f32[2,34,1]{2,1,0:T(8,128)S(1)} %get-tuple-element.80), channel_id=1, source_target_pairs={{0,1},{1,2},{2,3},{3,4},{4,5},{5,6},{6,7},{8,9},{9,10},{10,11},{11... | collective-permute-start | bytes 824 | tf_op jit(solution)/shard_map/ppermute | solution.py:23
  60.9 5.5 %collective-permute-start.15 = (f32[2,34,1]{2,1,0:T(8,128)S(1)}, f32[2,34,1]{2,1,0:T(8,128)S(1)}, u32[]{:S(2)}, u32[]{:S(2)}) collective-permute-start(f32[2,34,1]{2,1,0:T(8,128)S(1)} %get-tuple-element.81), channel_id=1, source_target_pairs={{1,0},{2,1},{3,2},{4,3},{5,4},{6,5},{7,6},{9,8},{10,9},{11,10},{12... | collective-permute-start | bytes 824 | tf_op jit(solution)/shard_map/ppermute | solution.py:26
  62.9 5.5 %collective-permute-start.9 = (f32[3,1,256]{2,1,0:T(1,128)S(1)}, f32[3,1,256]{2,1,0:T(1,128)S(1)}, u32[]{:S(2)}, u32[]{:S(2)}) collective-permute-start(f32[3,1,256]{2,1,0:T(1,128)S(1)} %get-tuple-element.109), channel_id=1, source_target_pairs={{8,0},{16,8},{24,16},{9,1},{17,9},{25,17},{10,2},{18,10},{26,18},{... | collective-permute-start | bytes 9224 | tf_op jit(solution)/shard_map/ppermute | solution.py:26
  68.5 6.5 %collective-permute-start.10 = (f32[3,34,1]{2,1,0:T(8,128)S(1)}, f32[3,34,1]{2,1,0:T(8,128)S(1)}, u32[]{:S(2)}, u32[]{:S(2)}) collective-permute-start(f32[3,34,1]{2,1,0:T(8,128)S(1)} %get-tuple-element.68), channel_id=1, source_target_pairs={{0,1},{1,2},{2,3},{3,4},{4,5},{5,6},{6,7},{8,9},{9,10},{10,11},{11... | collective-permute-start | bytes 1232 | tf_op jit(solution)/shard_map/ppermute | solution.py:23
  73.0 5.5 %collective-permute-start.11 = (f32[3,34,1]{2,1,0:T(8,128)S(1)}, f32[3,34,1]{2,1,0:T(8,128)S(1)}, u32[]{:S(2)}, u32[]{:S(2)}) collective-permute-start(f32[3,34,1]{2,1,0:T(8,128)S(1)} %get-tuple-element.69), channel_id=1, source_target_pairs={{1,0},{2,1},{3,2},{4,3},{5,4},{6,5},{7,6},{9,8},{10,9},{11,10},{12... | collective-permute-start | bytes 1232 | tf_op jit(solution)/shard_map/ppermute | solution.py:26
  78.9 5.4 %collective-permute-start.2 = (f32[4,130,1]{2,1,0:T(8,128)S(1)}, f32[4,130,1]{2,1,0:T(8,128)S(1)}, u32[]{:S(2)}, u32[]{:S(2)}) collective-permute-start(f32[4,130,1]{2,1,0:T(8,128)S(1)} %get-tuple-element.28), channel_id=1, source_target_pairs={{0,1},{1,2},{2,3},{3,4},{4,5},{5,6},{6,7},{8,9},{9,10},{10,11},{11... | collective-permute-start | bytes 6248 | tf_op jit(solution)/shard_map/ppermute | solution.py:23
  80.9 7.9 %collective-permute-start.3 = (f32[4,130,1]{2,1,0:T(8,128)S(1)}, f32[4,130,1]{2,1,0:T(8,128)S(1)}, u32[]{:S(2)}, u32[]{:S(2)}) collective-permute-start(f32[4,130,1]{2,1,0:T(8,128)S(1)} %get-tuple-element.29), channel_id=1, source_target_pairs={{1,0},{2,1},{3,2},{4,3},{5,4},{6,5},{7,6},{9,8},{10,9},{11,10},{12... | collective-permute-start | bytes 6248 | tf_op jit(solution)/shard_map/ppermute | solution.py:26
  89.4 0.9 copy-start.2
  90.5 6.0 %collective-permute-start.4 = (f32[4,1,256]{2,1,0:T(1,128)S(1)}, f32[4,1,256]{2,1,0:T(1,128)S(1)}, u32[]{:S(2)}, u32[]{:S(2)}) collective-permute-start(f32[4,1,256]{2,1,0:T(1,128)S(1)} %get-tuple-element.30), channel_id=1, source_target_pairs={{0,8},{8,16},{16,24},{1,9},{9,17},{17,25},{2,10},{10,18},{18,26},{... | collective-permute-start | bytes 12296 | tf_op jit(solution)/shard_map/ppermute | solution.py:23
  95.1 4.4 %collective-permute-start.5 = (f32[4,1,256]{2,1,0:T(1,128)S(1)}, f32[4,1,256]{2,1,0:T(1,128)S(1)}, u32[]{:S(2)}, u32[]{:S(2)}) collective-permute-start(f32[4,1,256]{2,1,0:T(1,128)S(1)} %get-tuple-element.31), channel_id=1, source_target_pairs={{8,0},{16,8},{24,16},{9,1},{17,9},{25,17},{10,2},{18,10},{26,18},{... | collective-permute-start | bytes 12296 | tf_op jit(solution)/shard_map/ppermute | solution.py:26
  99.6 29.0 %collective-permute-start.6 = (f32[4,130,1]{2,1,0:T(8,128)S(1)}, f32[4,130,1]{2,1,0:T(8,128)S(1)}, u32[]{:S(2)}, u32[]{:S(2)}) collective-permute-start(f32[4,130,1]{2,1,0:T(8,128)S(1)} %get-tuple-element.26), channel_id=1, source_target_pairs={{0,1},{1,2},{2,3},{3,4},{4,5},{5,6},{6,7},{8,9},{9,10},{10,11},{11... | collective-permute-start | bytes 6248 | tf_op jit(solution)/shard_map/ppermute | solution.py:23
  102.8 25.8 %collective-permute-start.7 = (f32[4,130,1]{2,1,0:T(8,128)S(1)}, f32[4,130,1]{2,1,0:T(8,128)S(1)}, u32[]{:S(2)}, u32[]{:S(2)}) collective-permute-start(f32[4,130,1]{2,1,0:T(8,128)S(1)} %get-tuple-element.27), channel_id=1, source_target_pairs={{1,0},{2,1},{3,2},{4,3},{5,4},{6,5},{7,6},{9,8},{10,9},{11,10},{12... | collective-permute-start | bytes 6248 | tf_op jit(solution)/shard_map/ppermute | solution.py:26
  129.7 0.7 copy-start.3
  154.4 0.6 copy-start.5
  276.0 4.4 %collective-permute-start.16 = (f32[3,1,256]{2,1,0:T(1,128)S(1)}, f32[3,1,256]{2,1,0:T(1,128)S(1)}, u32[]{:S(2)}, u32[]{:S(2)}) collective-permute-start(f32[3,1,256]{2,1,0:T(1,128)S(1)} %get-tuple-element.78), channel_id=1, source_target_pairs={{0,8},{8,16},{16,24},{1,9},{9,17},{17,25},{2,10},{10,18},{18,26},{... | collective-permute-start | bytes 9224 | tf_op jit(solution)/shard_map/ppermute | solution.py:23
  279.1 4.3 %collective-permute-start.17 = (f32[3,1,256]{2,1,0:T(1,128)S(1)}, f32[3,1,256]{2,1,0:T(1,128)S(1)}, u32[]{:S(2)}, u32[]{:S(2)}) collective-permute-start(f32[3,1,256]{2,1,0:T(1,128)S(1)} %get-tuple-element.79), channel_id=1, source_target_pairs={{8,0},{16,8},{24,16},{9,1},{17,9},{25,17},{10,2},{18,10},{26,18},{... | collective-permute-start | bytes 9224 | tf_op jit(solution)/shard_map/ppermute | solution.py:26
  283.5 9.1 %collective-permute-start.18 = (f32[3,34,1]{2,1,0:T(8,128)S(1)}, f32[3,34,1]{2,1,0:T(8,128)S(1)}, u32[]{:S(2)}, u32[]{:S(2)}) collective-permute-start(f32[3,34,1]{2,1,0:T(8,128)S(1)} %get-tuple-element.64), channel_id=1, source_target_pairs={{0,1},{1,2},{2,3},{3,4},{4,5},{5,6},{6,7},{8,9},{9,10},{10,11},{11... | collective-permute-start | bytes 1232 | tf_op jit(solution)/shard_map/ppermute | solution.py:23
  290.7 5.5 %collective-permute-start.19 = (f32[3,34,1]{2,1,0:T(8,128)S(1)}, f32[3,34,1]{2,1,0:T(8,128)S(1)}, u32[]{:S(2)}, u32[]{:S(2)}) collective-permute-start(f32[3,34,1]{2,1,0:T(8,128)S(1)} %get-tuple-element.65), channel_id=1, source_target_pairs={{1,0},{2,1},{3,2},{4,3},{5,4},{6,5},{7,6},{9,8},{10,9},{11,10},{12... | collective-permute-start | bytes 1232 | tf_op jit(solution)/shard_map/ppermute | solution.py:26
  297.7 5.3 %collective-permute-start.20 = (f32[3,1,256]{2,1,0:T(1,128)S(1)}, f32[3,1,256]{2,1,0:T(1,128)S(1)}, u32[]{:S(2)}, u32[]{:S(2)}) collective-permute-start(f32[3,1,256]{2,1,0:T(1,128)S(1)} %get-tuple-element.76), channel_id=1, source_target_pairs={{0,8},{8,16},{16,24},{1,9},{9,17},{17,25},{2,10},{10,18},{18,26},{... | collective-permute-start | bytes 9224 | tf_op jit(solution)/shard_map/ppermute | solution.py:23
  301.7 4.3 %collective-permute-start.21 = (f32[3,1,256]{2,1,0:T(1,128)S(1)}, f32[3,1,256]{2,1,0:T(1,128)S(1)}, u32[]{:S(2)}, u32[]{:S(2)}) collective-permute-start(f32[3,1,256]{2,1,0:T(1,128)S(1)} %get-tuple-element.77), channel_id=1, source_target_pairs={{8,0},{16,8},{24,16},{9,1},{17,9},{25,17},{10,2},{18,10},{26,18},{... | collective-permute-start | bytes 9224 | tf_op jit(solution)/shard_map/ppermute | solution.py:26
  306.1 5.2 %collective-permute-start.22 = (f32[3,34,1]{2,1,0:T(8,128)S(1)}, f32[3,34,1]{2,1,0:T(8,128)S(1)}, u32[]{:S(2)}, u32[]{:S(2)}) collective-permute-start(f32[3,34,1]{2,1,0:T(8,128)S(1)} %get-tuple-element.62), channel_id=1, source_target_pairs={{0,1},{1,2},{2,3},{3,4},{4,5},{5,6},{6,7},{8,9},{9,10},{10,11},{11... | collective-permute-start | bytes 1232 | tf_op jit(solution)/shard_map/ppermute | solution.py:23
  309.4 5.5 %collective-permute-start.23 = (f32[3,34,1]{2,1,0:T(8,128)S(1)}, f32[3,34,1]{2,1,0:T(8,128)S(1)}, u32[]{:S(2)}, u32[]{:S(2)}) collective-permute-start(f32[3,34,1]{2,1,0:T(8,128)S(1)} %get-tuple-element.63), channel_id=1, source_target_pairs={{1,0},{2,1},{3,2},{4,3},{5,4},{6,5},{7,6},{9,8},{10,9},{11,10},{12... | collective-permute-start | bytes 1232 | tf_op jit(solution)/shard_map/ppermute | solution.py:26
  316.4 3.9 %collective-permute-start.24 = (f32[3,1,256]{2,1,0:T(1,128)S(1)}, f32[3,1,256]{2,1,0:T(1,128)S(1)}, u32[]{:S(2)}, u32[]{:S(2)}) collective-permute-start(f32[3,1,256]{2,1,0:T(1,128)S(1)} %get-tuple-element.74), channel_id=1, source_target_pairs={{0,8},{8,16},{16,24},{1,9},{9,17},{17,25},{2,10},{10,18},{18,26},{... | collective-permute-start | bytes 9224 | tf_op jit(solution)/shard_map/ppermute | solution.py:23
  319.0 4.3 %collective-permute-start.25 = (f32[3,1,256]{2,1,0:T(1,128)S(1)}, f32[3,1,256]{2,1,0:T(1,128)S(1)}, u32[]{:S(2)}, u32[]{:S(2)}) collective-permute-start(f32[3,1,256]{2,1,0:T(1,128)S(1)} %get-tuple-element.75), channel_id=1, source_target_pairs={{8,0},{16,8},{24,16},{9,1},{17,9},{25,17},{10,2},{18,10},{26,18},{... | collective-permute-start | bytes 9224 | tf_op jit(solution)/shard_map/ppermute | solution.py:26
  323.4 5.2 %collective-permute-start.26 = (f32[3,34,1]{2,1,0:T(8,128)S(1)}, f32[3,34,1]{2,1,0:T(8,128)S(1)}, u32[]{:S(2)}, u32[]{:S(2)}) collective-permute-start(f32[3,34,1]{2,1,0:T(8,128)S(1)} %get-tuple-element.60), channel_id=1, source_target_pairs={{0,1},{1,2},{2,3},{3,4},{4,5},{5,6},{6,7},{8,9},{9,10},{10,11},{11... | collective-permute-start | bytes 1232 | tf_op jit(solution)/shard_map/ppermute | solution.py:23
  326.7 5.5 %collective-permute-start.27 = (f32[3,34,1]{2,1,0:T(8,128)S(1)}, f32[3,34,1]{2,1,0:T(8,128)S(1)}, u32[]{:S(2)}, u32[]{:S(2)}) collective-permute-start(f32[3,34,1]{2,1,0:T(8,128)S(1)} %get-tuple-element.61), channel_id=1, source_target_pairs={{1,0},{2,1},{3,2},{4,3},{5,4},{6,5},{7,6},{9,8},{10,9},{11,10},{12... | collective-permute-start | bytes 1232 | tf_op jit(solution)/shard_map/ppermute | solution.py:26
  333.7 3.9 %collective-permute-start.28 = (f32[3,1,256]{2,1,0:T(1,128)S(1)}, f32[3,1,256]{2,1,0:T(1,128)S(1)}, u32[]{:S(2)}, u32[]{:S(2)}) collective-permute-start(f32[3,1,256]{2,1,0:T(1,128)S(1)} %get-tuple-element.72), channel_id=1, source_target_pairs={{0,8},{8,16},{16,24},{1,9},{9,17},{17,25},{2,10},{10,18},{18,26},{... | collective-permute-start | bytes 9224 | tf_op jit(solution)/shard_map/ppermute | solution.py:23
  336.2 4.3 %collective-permute-start.29 = (f32[3,1,256]{2,1,0:T(1,128)S(1)}, f32[3,1,256]{2,1,0:T(1,128)S(1)}, u32[]{:S(2)}, u32[]{:S(2)}) collective-permute-start(f32[3,1,256]{2,1,0:T(1,128)S(1)} %get-tuple-element.73), channel_id=1, source_target_pairs={{8,0},{16,8},{24,16},{9,1},{17,9},{25,17},{10,2},{18,10},{26,18},{... | collective-permute-start | bytes 9224 | tf_op jit(solution)/shard_map/ppermute | solution.py:26
  340.7 5.2 %collective-permute-start.30 = (f32[3,34,1]{2,1,0:T(8,128)S(1)}, f32[3,34,1]{2,1,0:T(8,128)S(1)}, u32[]{:S(2)}, u32[]{:S(2)}) collective-permute-start(f32[3,34,1]{2,1,0:T(8,128)S(1)} %get-tuple-element.58), channel_id=1, source_target_pairs={{0,1},{1,2},{2,3},{3,4},{4,5},{5,6},{6,7},{8,9},{9,10},{10,11},{11... | collective-permute-start | bytes 1232 | tf_op jit(solution)/shard_map/ppermute | solution.py:23
  344.0 5.5 %collective-permute-start.31 = (f32[3,34,1]{2,1,0:T(8,128)S(1)}, f32[3,34,1]{2,1,0:T(8,128)S(1)}, u32[]{:S(2)}, u32[]{:S(2)}) collective-permute-start(f32[3,34,1]{2,1,0:T(8,128)S(1)} %get-tuple-element.59), channel_id=1, source_target_pairs={{1,0},{2,1},{3,2},{4,3},{5,4},{6,5},{7,6},{9,8},{10,9},{11,10},{12... | collective-permute-start | bytes 1232 | tf_op jit(solution)/shard_map/ppermute | solution.py:26
  351.0 3.9 %collective-permute-start.32 = (f32[3,1,256]{2,1,0:T(1,128)S(1)}, f32[3,1,256]{2,1,0:T(1,128)S(1)}, u32[]{:S(2)}, u32[]{:S(2)}) collective-permute-start(f32[3,1,256]{2,1,0:T(1,128)S(1)} %get-tuple-element.70), channel_id=1, source_target_pairs={{0,8},{8,16},{16,24},{1,9},{9,17},{17,25},{2,10},{10,18},{18,26},{... | collective-permute-start | bytes 9224 | tf_op jit(solution)/shard_map/ppermute | solution.py:23
  353.5 4.3 %collective-permute-start.33 = (f32[3,1,256]{2,1,0:T(1,128)S(1)}, f32[3,1,256]{2,1,0:T(1,128)S(1)}, u32[]{:S(2)}, u32[]{:S(2)}) collective-permute-start(f32[3,1,256]{2,1,0:T(1,128)S(1)} %get-tuple-element.71), channel_id=1, source_target_pairs={{8,0},{16,8},{24,16},{9,1},{17,9},{25,17},{10,2},{18,10},{26,18},{... | collective-permute-start | bytes 9224 | tf_op jit(solution)/shard_map/ppermute | solution.py:26
  357.9 5.3 %collective-permute-start.34 = (f32[3,34,1]{2,1,0:T(8,128)S(1)}, f32[3,34,1]{2,1,0:T(8,128)S(1)}, u32[]{:S(2)}, u32[]{:S(2)}) collective-permute-start(f32[3,34,1]{2,1,0:T(8,128)S(1)} %get-tuple-element.56), channel_id=1, source_target_pairs={{0,1},{1,2},{2,3},{3,4},{4,5},{5,6},{6,7},{8,9},{9,10},{10,11},{11... | collective-permute-start | bytes 1232 | tf_op jit(solution)/shard_map/ppermute | solution.py:23
  361.3 5.5 %collective-permute-start.35 = (f32[3,34,1]{2,1,0:T(8,128)S(1)}, f32[3,34,1]{2,1,0:T(8,128)S(1)}, u32[]{:S(2)}, u32[]{:S(2)}) collective-permute-start(f32[3,34,1]{2,1,0:T(8,128)S(1)} %get-tuple-element.57), channel_id=1, source_target_pairs={{1,0},{2,1},{3,2},{4,3},{5,4},{6,5},{7,6},{9,8},{10,9},{11,10},{12... | collective-permute-start | bytes 1232 | tf_op jit(solution)/shard_map/ppermute | solution.py:26
Sparse Core Ops, SparseCore 0:
  155.1 119.8 all-reduce.2
where the time goes:
time: 378 us; the launch traced here: 376 us
  waiting for transfers between devices  169 us (45%)
  starting transfers between devices  96.1 us (25%)
  local copies, waits for them, and re-layouts  75.5 us (20%)
  other arithmetic  20.3 us (5%)
  between operations  15.2 us (4%)
    psum x1, waiting for transfers between devices, per_device(): summed = lax.psum(per_step, ('rows', 'cols'))  120 us
    ppermute x18, starting transfers between devices, padded_2(): lax.ppermute(lax.slice_in_dim(block, block.shape[dim] - width, None, axis...  66.7 us
    ppermute x18, waiting for transfers between devices, padded_2(): lax.ppermute(lax.slice_in_dim(block, 0, width, axis=dim), axis, backward)  48.1 us
    gather x3, local copies, waits for them, and re-layouts, sample(): jnp.take(velocity.reshape(-1), flat_index) * owned_weight  35.3 us
    gather x3, local copies, waits for them, and re-layouts, sample(): jnp.take(surface.reshape(-1), flat_index) * owned_weight  35.3 us
    ppermute x18, starting transfers between devices, padded_2(): lax.ppermute(lax.slice_in_dim(block, 0, width, axis=dim), axis, backward)  29.4 us
  transfers between devices with their start and end apart: 37, of which 17 were waited for; matrix products, arithmetic and copies ran while one was open for 15% of the time, Pallas kernels for 0%

commit v1 on v0

--- a/solution.py
+++ b/solution.py
@@ -129,7 +129,7 @@
         sampled.append(sample(surface, rows_flux))
     levels_stack = jnp.stack(sampled)
     per_step = jnp.stack([blend(levels_stack, fine_index) for fine_index in range(FSTEPS)])
-    summed = lax.psum(per_step, ("rows", "cols"))
+    summed = lax.psum(lax.psum(per_step, "cols"), "rows")
     boundary = lax.dynamic_slice_in_dim(summed, col_index * fine_cols_dev, fine_cols_dev, 2)
     roughness = jnp.zeros_like(f_bed)
     for class_index in range(NCLASS):

time: 378 us -> 354 us (0.937)
  waiting for transfers between devices: 169 us -> 147 us
    psum x1 -> x2, waiting for transfers between devices: 120 us -> 97.3 us  [per_device(): summed = lax.psum(lax.psum(per_step, 'cols'), 'rows')]
  transfers between devices with their start and end apart: 37 -> 38, of which waited for: 17 -> 18; matrix products, arithmetic and copies ran while one was open for 15% -> 16% of each run, Pallas kernels for 0% -> 0%
where the time goes in v1:
time: 354 us; the launch traced here: 352 us
  waiting for transfers between devices  147 us (42%)
  starting transfers between devices  94.4 us (27%)
  local copies, waits for them, and re-layouts  75.5 us (21%)
  other arithmetic  20.3 us (6%)
  between operations  15.2 us (4%)
    psum x2, waiting for transfers between devices, per_device(): summed = lax.psum(lax.psum(per_step, 'cols'), 'rows')  97.3 us
    ppermute x18, starting transfers between devices, padded_2(): lax.ppermute(lax.slice_in_dim(block, block.shape[dim] - width, None, axis...  64.9 us
    ppermute x18, waiting for transfers between devices, padded_2(): lax.ppermute(lax.slice_in_dim(block, 0, width, axis=dim), axis, backward)  48.3 us
    gather x3, local copies, waits for them, and re-layouts, sample(): jnp.take(velocity.reshape(-1), flat_index) * owned_weight  35.3 us
    gather x3, local copies, waits for them, and re-layouts, sample(): jnp.take(surface.reshape(-1), flat_index) * owned_weight  35.3 us
    ppermute x18, starting transfers between devices, padded_2(): lax.ppermute(lax.slice_in_dim(block, 0, width, axis=dim), axis, backward)  29.4 us
  transfers between devices with their start and end apart: 38, of which 18 were waited for; matrix products, arithmetic and copies ran while one was open for 16% of the time, Pallas kernels for 0%

profile of v1, /device:TPU:1, one launch (start us, length us, event | category | flops | bytes accessed | tf_op | source)
XLA Modules:
  0.0 352.1 jit_solution(9115187169508762083)
XLA Ops:
  7.2 1.1 fusion.22
  8.4 3.9 %collective-permute-start = (f32[4,1,256]{2,1,0:T(1,128)S(1)}, f32[4,1,256]{2,1,0:T(1,128)S(1)}, u32[]{:S(2)}, u32[]{:S(2)}) collective-permute-start(f32[4,1,256]{2,1,0:T(1,128)S(1)} %get-tuple-element.32), channel_id=1, source_target_pairs={{0,8},{8,16},{16,24},{1,9},{9,17},{17,25},{2,10},{10,18},{18,26},{... | collective-permute-start | bytes 12296 | tf_op jit(solution)/shard_map/ppermute | solution.py:23
  12.4 1.3 collective-permute-start.1
  14.4 7.0 %select_bitcast_fusion = f32[1,32,256]{2,1,0:T(8,128)S(1)} fusion(s32[32,256]{1,0:T(8,128)S(1)} %copy-done.9, f32[]{:T(128)} %bitcast.27, f32[]{:T(128)} %bitcast.26, f32[]{:T(128)} %bitcast.25, f32[]{:T(128)} %bitcast.24, f32[]{:T(128)} %bitcast.23, f32[]{:T(128)} %bitcast.22, f32[]{:T(128)} %bitcast.21, f32[]{:T(128)} %bitcast.20, f32[]{:T(128)} %bitcast.19, ...), kind=kLoop, calls=%fused_computation.156 | loop fusion | flops 180224 | bytes 65580 | tf_op jit(solution)/shard_map/stack | solution.py:147
  21.4 4.0 %collective-permute-start.12 = (f32[2,1,256]{2,1,0:T(1,128)S(1)}, f32[2,1,256]{2,1,0:T(1,128)S(1)}, u32[]{:S(2)}, u32[]{:S(2)}) collective-permute-start(f32[2,1,256]{2,1,0:T(1,128)S(1)} %get-tuple-element.82), channel_id=1, source_target_pairs={{0,8},{8,16},{16,24},{1,9},{9,17},{17,25},{2,10},{10,18},{18,26},{... | collective-permute-start | bytes 6152 | tf_op jit(solution)/shard_map/ppermute | solution.py:23
  25.4 1.3 collective-permute-start.13
  26.8 4.7 %collective-permute-start.8 = (f32[3,1,256]{2,1,0:T(1,128)S(1)}, f32[3,1,256]{2,1,0:T(1,128)S(1)}, u32[]{:S(2)}, u32[]{:S(2)}) collective-permute-start(f32[3,1,256]{2,1,0:T(1,128)S(1)} %get-tuple-element.108), channel_id=1, source_target_pairs={{0,8},{8,16},{16,24},{1,9},{9,17},{17,25},{2,10},{10,18},{18,26},{... | collective-permute-start | bytes 9224 | tf_op jit(solution)/shard_map/ppermute | solution.py:23
  32.3 11.8 %gather_fusion.1 = f32[2048]{0:T(1024)S(1)} fusion(f32[32768]{0:T(1024)S(1)} %bitcast.271, s32[2048]{0:T(1024)S(1)} %get-tuple-element.10), kind=kCustom, calls=%fused_computation.1.clone | custom fusion | bytes 24576 | tf_op jit(solution)/shard_map/jit(_take)/gather | solution.py:117
  44.1 11.8 %gather_fusion = f32[2048]{0:T(1024)S(1)} fusion(f32[32768]{0:T(1024)S(1)} %bitcast.272, s32[2048]{0:T(1024)S(1)} %get-tuple-element.10), kind=kCustom, calls=%fused_computation.clone | custom fusion | bytes 24576 | tf_op jit(solution)/shard_map/jit(_take)/gather | solution.py:116
  56.0 4.9 %collective-permute-start.14 = (f32[2,34,1]{2,1,0:T(8,128)S(1)}, f32[2,34,1]{2,1,0:T(8,128)S(1)}, u32[]{:S(2)}, u32[]{:S(2)}) collective-permute-start(f32[2,34,1]{2,1,0:T(8,128)S(1)} %get-tuple-element.80), channel_id=1, source_target_pairs={{0,1},{1,2},{2,3},{3,4},{4,5},{5,6},{6,7},{8,9},{9,10},{10,11},{11... | collective-permute-start | bytes 824 | tf_op jit(solution)/shard_map/ppermute | solution.py:23
  60.9 1.9 collective-permute-start.15
  62.9 1.3 collective-permute-start.9
  64.2 2.3 collective-permute-done.15
  66.6 1.8 collective-permute-done.9
  68.5 4.5 %collective-permute-start.10 = (f32[3,34,1]{2,1,0:T(8,128)S(1)}, f32[3,34,1]{2,1,0:T(8,128)S(1)}, u32[]{:S(2)}, u32[]{:S(2)}) collective-permute-start(f32[3,34,1]{2,1,0:T(8,128)S(1)} %get-tuple-element.68), channel_id=1, source_target_pairs={{0,1},{1,2},{2,3},{3,4},{4,5},{5,6},{6,7},{8,9},{9,10},{10,11},{11... | collective-permute-start | bytes 1232 | tf_op jit(solution)/shard_map/ppermute | solution.py:23
  73.0 1.9 collective-permute-start.11
  75.0 3.6 %collective-permute-done.11 = f32[3,34,1]{2,1,0:T(8,128)S(1)} collective-permute-done((f32[3,34,1]{2,1,0:T(8,128)S(1)}, f32[3,34,1]{2,1,0:T(8,128)S(1)}, u32[]{:S(2)}, u32[]{:S(2)}) %collective-permute-start.11) | collective-permute-done | bytes 440 | tf_op jit(solution)/shard_map/ppermute | solution.py:26
  78.9 1.9 collective-permute-start.2
  80.8 2.4 collective-permute-start.3
  83.3 1.0 collective-permute-done.2
  84.3 4.4 %collective-permute-done.3 = f32[4,130,1]{2,1,0:T(8,128)S(1)} collective-permute-done((f32[4,130,1]{2,1,0:T(8,128)S(1)}, f32[4,130,1]{2,1,0:T(8,128)S(1)}, u32[]{:S(2)}, u32[]{:S(2)}) %collective-permute-start.3) | collective-permute-done | bytes 2112 | tf_op jit(solution)/shard_map/ppermute | solution.py:26
  90.5 4.5 %collective-permute-start.4 = (f32[4,1,256]{2,1,0:T(1,128)S(1)}, f32[4,1,256]{2,1,0:T(1,128)S(1)}, u32[]{:S(2)}, u32[]{:S(2)}) collective-permute-start(f32[4,1,256]{2,1,0:T(1,128)S(1)} %get-tuple-element.30), channel_id=1, source_target_pairs={{0,8},{8,16},{16,24},{1,9},{9,17},{17,25},{2,10},{10,18},{18,26},{... | collective-permute-start | bytes 12296 | tf_op jit(solution)/shard_map/ppermute | solution.py:23
  95.0 1.3 collective-permute-start.5
  96.4 3.0 collective-permute-done.5
  99.6 3.2 collective-permute-start.6
  102.8 1.9 collective-permute-start.7
  104.9 11.8 %gather_fusion.2 = f32[2048]{0:T(1024)S(1)} fusion(f32[32768]{0:T(1024)S(1)} %bitcast.275, s32[2048]{0:T(1024)S(1)} %get-tuple-element.10), kind=kCustom, calls=%fused_computation.2.clone | custom fusion | bytes 24576 | tf_op jit(solution)/shard_map/jit(_take)/gather | solution.py:116
  116.8 11.8 %gather_fusion.3 = f32[2048]{0:T(1024)S(1)} fusion(f32[32768]{0:T(1024)S(1)} %bitcast.274, s32[2048]{0:T(1024)S(1)} %get-tuple-element.10), kind=kCustom, calls=%fused_computation.3.clone | custom fusion | bytes 24576 | tf_op jit(solution)/shard_map/jit(_take)/gather | solution.py:117
  130.4 11.8 %gather_fusion.4 = f32[2048]{0:T(1024)S(1)} fusion(f32[32768]{0:T(1024)S(1)} %bitcast.276, s32[2048]{0:T(1024)S(1)} %get-tuple-element.10), kind=kCustom, calls=%fused_computation.4.clone | custom fusion | bytes 24576 | tf_op jit(solution)/shard_map/jit(_take)/gather | solution.py:116
  142.2 11.8 %gather_fusion.5 = f32[2048]{0:T(1024)S(1)} fusion(f32[32768]{0:T(1024)S(1)} %bitcast.273, s32[2048]{0:T(1024)S(1)} %get-tuple-element.10), kind=kCustom, calls=%fused_computation.5.clone | custom fusion | bytes 24576 | tf_op jit(solution)/shard_map/jit(_take)/gather | solution.py:117
  155.2 50.5 %all-reduce.4.cloned.1.call-done = f32[6,2,2048]{2,1,0:T(2,128)} async-done(((f32[6,2,2048]{2,1,0:T(2,128)}), f32[6,2,2048]{2,1,0:T(2,128)}) %all-reduce.4.cloned.1.call-update) | async-done | bytes 98320 | tf_op jit(solution)/shard_map/psum | solution.py:132
  205.8 46.8 %all-reduce.6.cloned.1.call-done = f32[6,2,2048]{2,1,0:T(2,128)} async-done(((f32[6,2,2048]{2,1,0:T(2,128)}), f32[6,2,2048]{2,1,0:T(2,128)}) %all-reduce.6.cloned.1.call-update) | async-done | bytes 98320 | tf_op jit(solution)/shard_map/psum | solution.py:132
  253.5 3.0 collective-permute-start.16
  256.5 1.3 collective-permute-start.17
  257.8 3.0 collective-permute-done.17
  261.0 5.6 %collective-permute-start.18 = (f32[3,34,1]{2,1,0:T(8,128)S(1)}, f32[3,34,1]{2,1,0:T(8,128)S(1)}, u32[]{:S(2)}, u32[]{:S(2)}) collective-permute-start(f32[3,34,1]{2,1,0:T(8,128)S(1)} %get-tuple-element.64), channel_id=1, source_target_pairs={{0,1},{1,2},{2,3},{3,4},{4,5},{5,6},{6,7},{8,9},{9,10},{10,11},{11... | collective-permute-start | bytes 1232 | tf_op jit(solution)/shard_map/ppermute | solution.py:23
  266.5 1.9 collective-permute-start.19
  268.5 3.6 %collective-permute-done.19 = f32[3,34,1]{2,1,0:T(8,128)S(1)} collective-permute-done((f32[3,34,1]{2,1,0:T(8,128)S(1)}, f32[3,34,1]{2,1,0:T(8,128)S(1)}, u32[]{:S(2)}, u32[]{:S(2)}) %collective-permute-start.19) | collective-permute-done | bytes 440 | tf_op jit(solution)/shard_map/ppermute | solution.py:26
  272.6 0.8 broadcast_select_fusion.4
  273.5 3.9 %collective-permute-start.20 = (f32[3,1,256]{2,1,0:T(1,128)S(1)}, f32[3,1,256]{2,1,0:T(1,128)S(1)}, u32[]{:S(2)}, u32[]{:S(2)}) collective-permute-start(f32[3,1,256]{2,1,0:T(1,128)S(1)} %get-tuple-element.76), channel_id=1, source_target_pairs={{0,8},{8,16},{16,24},{1,9},{9,17},{17,25},{2,10},{10,18},{18,26},{... | collective-permute-start | bytes 9224 | tf_op jit(solution)/shard_map/ppermute | solution.py:23
  277.5 1.3 collective-permute-start.21
  278.8 3.0 collective-permute-done.21
  281.9 3.3 collective-permute-start.22
  285.2 1.9 collective-permute-start.23
  287.1 3.6 %collective-permute-done.23 = f32[3,34,1]{2,1,0:T(8,128)S(1)} collective-permute-done((f32[3,34,1]{2,1,0:T(8,128)S(1)}, f32[3,34,1]{2,1,0:T(8,128)S(1)}, u32[]{:S(2)}, u32[]{:S(2)}) %collective-permute-start.23) | collective-permute-done | bytes 440 | tf_op jit(solution)/shard_map/ppermute | solution.py:26
  291.2 0.8 broadcast_select_fusion.3
  292.2 2.5 collective-permute-start.24
  294.7 1.3 collective-permute-start.25
  296.0 3.0 collective-permute-done.25
  299.2 3.3 collective-permute-start.26
  302.5 1.9 collective-permute-start.27
  304.4 3.6 %collective-permute-done.27 = f32[3,34,1]{2,1,0:T(8,128)S(1)} collective-permute-done((f32[3,34,1]{2,1,0:T(8,128)S(1)}, f32[3,34,1]{2,1,0:T(8,128)S(1)}, u32[]{:S(2)}, u32[]{:S(2)}) %collective-permute-start.27) | collective-permute-done | bytes 440 | tf_op jit(solution)/shard_map/ppermute | solution.py:26
  309.5 2.5 collective-permute-start.28
  312.0 1.3 collective-permute-start.29
  313.3 3.0 collective-permute-done.29
  316.4 3.3 collective-permute-start.30
  319.8 1.9 collective-permute-start.31
  321.7 3.6 %collective-permute-done.31 = f32[3,34,1]{2,1,0:T(8,128)S(1)} collective-permute-done((f32[3,34,1]{2,1,0:T(8,128)S(1)}, f32[3,34,1]{2,1,0:T(8,128)S(1)}, u32[]{:S(2)}, u32[]{:S(2)}) %collective-permute-start.31) | collective-permute-done | bytes 440 | tf_op jit(solution)/shard_map/ppermute | solution.py:26
  326.7 2.5 collective-permute-start.32
  329.3 1.3 collective-permute-start.33
  330.6 3.0 collective-permute-done.33
  333.7 3.3 collective-permute-start.34
  337.0 1.9 collective-permute-start.35
  339.0 3.6 %collective-permute-done.35 = f32[3,34,1]{2,1,0:T(8,128)S(1)} collective-permute-done((f32[3,34,1]{2,1,0:T(8,128)S(1)}, f32[3,34,1]{2,1,0:T(8,128)S(1)}, u32[]{:S(2)}, u32[]{:S(2)}) %collective-permute-start.35) | collective-permute-done | bytes 440 | tf_op jit(solution)/shard_map/ppermute | solution.py:26
  (153 shorter events, 15.5 us)
Async XLA Ops:
  7.2 1.2 copy-start
  7.2 1.2 copy-start.1
  7.2 198.6 %all-reduce.4.cloned.1.call-start = ((), (), s32[]{:S(2)}) async-start(), calls=%async_computation | async-start | bytes 196608 | tf_op jit(solution)/shard_map/psum | solution.py:132
  8.4 5.3 %copy-start.6 = (f32[11]{0:T(128)S(1)}, f32[11]{0:T(128)}, u32[]{:S(2)}) copy-start(f32[11]{0:T(128)} %param.18) | copy-start | bytes 136
  8.4 6.0 %copy-start.9 = (s32[32,256]{1,0:T(8,128)S(1)}, s32[32,256]{1,0:T(8,128)}, u32[]{:S(2)}) copy-start(s32[32,256]{1,0:T(8,128)} %param.17) | copy-start | bytes 98308
  8.4 70.3 %collective-permute-start = (f32[4,1,256]{2,1,0:T(1,128)S(1)}, f32[4,1,256]{2,1,0:T(1,128)S(1)}, u32[]{:S(2)}, u32[]{:S(2)}) collective-permute-start(f32[4,1,256]{2,1,0:T(1,128)S(1)} %get-tuple-element.32), channel_id=1, source_target_pairs={{0,8},{8,16},{16,24},{1,9},{9,17},{17,25},{2,10},{10,18},{18,26},{... | collective-permute-start | bytes 12296 | tf_op jit(solution)/shard_map/ppermute | solution.py:23
  12.4 66.3 %collective-permute-start.1 = (f32[4,1,256]{2,1,0:T(1,128)S(1)}, f32[4,1,256]{2,1,0:T(1,128)S(1)}, u32[]{:S(2)}, u32[]{:S(2)}) collective-permute-start(f32[4,1,256]{2,1,0:T(1,128)S(1)} %get-tuple-element.33), channel_id=1, source_target_pairs={{8,0},{16,8},{24,16},{9,1},{17,9},{25,17},{10,2},{18,10},{26,18},{... | collective-permute-start | bytes 12296 | tf_op jit(solution)/shard_map/ppermute | solution.py:26
  14.4 7.0 %copy-start.4 = (f32[32,256]{1,0:T(8,128)S(1)}, f32[32,256]{1,0:T(8,128)}, u32[]{:S(2)}) copy-start(f32[32,256]{1,0:T(8,128)} %param.14) | copy-start | bytes 98308
  21.4 5.3 %copy-start.7 = (f32[32,256]{1,0:T(8,128)S(1)}, f32[32,256]{1,0:T(8,128)}, u32[]{:S(2)}) copy-start(f32[32,256]{1,0:T(8,128)} %param.15) | copy-start | bytes 98308
  21.4 5.3 %copy-start.8 = (s32[32,256]{1,0:T(8,128)S(1)}, s32[32,256]{1,0:T(8,128)}, u32[]{:S(2)}) copy-start(s32[32,256]{1,0:T(8,128)} %param.16) | copy-start | bytes 98308
  21.4 34.5 %collective-permute-start.12 = (f32[2,1,256]{2,1,0:T(1,128)S(1)}, f32[2,1,256]{2,1,0:T(1,128)S(1)}, u32[]{:S(2)}, u32[]{:S(2)}) collective-permute-start(f32[2,1,256]{2,1,0:T(1,128)S(1)} %get-tuple-element.82), channel_id=1, source_target_pairs={{0,8},{8,16},{16,24},{1,9},{9,17},{17,25},{2,10},{10,18},{18,26},{... | collective-permute-start | bytes 6152 | tf_op jit(solution)/shard_map/ppermute | solution.py:23
  25.4 30.5 %collective-permute-start.13 = (f32[2,1,256]{2,1,0:T(1,128)S(1)}, f32[2,1,256]{2,1,0:T(1,128)S(1)}, u32[]{:S(2)}, u32[]{:S(2)}) collective-permute-start(f32[2,1,256]{2,1,0:T(1,128)S(1)} %get-tuple-element.83), channel_id=1, source_target_pairs={{8,0},{16,8},{24,16},{9,1},{17,9},{25,17},{10,2},{18,10},{26,18},{... | collective-permute-start | bytes 6152 | tf_op jit(solution)/shard_map/ppermute | solution.py:26
  26.8 39.8 %collective-permute-start.8 = (f32[3,1,256]{2,1,0:T(1,128)S(1)}, f32[3,1,256]{2,1,0:T(1,128)S(1)}, u32[]{:S(2)}, u32[]{:S(2)}) collective-permute-start(f32[3,1,256]{2,1,0:T(1,128)S(1)} %get-tuple-element.108), channel_id=1, source_target_pairs={{0,8},{8,16},{16,24},{1,9},{9,17},{17,25},{2,10},{10,18},{18,26},{... | collective-permute-start | bytes 9224 | tf_op jit(solution)/shard_map/ppermute | solution.py:23
  31.4 0.7 copy-start.10
  56.0 6.8 %collective-permute-start.14 = (f32[2,34,1]{2,1,0:T(8,128)S(1)}, f32[2,34,1]{2,1,0:T(8,128)S(1)}, u32[]{:S(2)}, u32[]{:S(2)}) collective-permute-start(f32[2,34,1]{2,1,0:T(8,128)S(1)} %get-tuple-element.80), channel_id=1, source_target_pairs={{0,1},{1,2},{2,3},{3,4},{4,5},{5,6},{6,7},{8,9},{9,10},{10,11},{11... | collective-permute-start | bytes 824 | tf_op jit(solution)/shard_map/ppermute | solution.py:23
  60.9 5.5 %collective-permute-start.15 = (f32[2,34,1]{2,1,0:T(8,128)S(1)}, f32[2,34,1]{2,1,0:T(8,128)S(1)}, u32[]{:S(2)}, u32[]{:S(2)}) collective-permute-start(f32[2,34,1]{2,1,0:T(8,128)S(1)} %get-tuple-element.81), channel_id=1, source_target_pairs={{1,0},{2,1},{3,2},{4,3},{5,4},{6,5},{7,6},{9,8},{10,9},{11,10},{12... | collective-permute-start | bytes 824 | tf_op jit(solution)/shard_map/ppermute | solution.py:26
  62.9 5.5 %collective-permute-start.9 = (f32[3,1,256]{2,1,0:T(1,128)S(1)}, f32[3,1,256]{2,1,0:T(1,128)S(1)}, u32[]{:S(2)}, u32[]{:S(2)}) collective-permute-start(f32[3,1,256]{2,1,0:T(1,128)S(1)} %get-tuple-element.109), channel_id=1, source_target_pairs={{8,0},{16,8},{24,16},{9,1},{17,9},{25,17},{10,2},{18,10},{26,18},{... | collective-permute-start | bytes 9224 | tf_op jit(solution)/shard_map/ppermute | solution.py:26
  68.5 6.5 %collective-permute-start.10 = (f32[3,34,1]{2,1,0:T(8,128)S(1)}, f32[3,34,1]{2,1,0:T(8,128)S(1)}, u32[]{:S(2)}, u32[]{:S(2)}) collective-permute-start(f32[3,34,1]{2,1,0:T(8,128)S(1)} %get-tuple-element.68), channel_id=1, source_target_pairs={{0,1},{1,2},{2,3},{3,4},{4,5},{5,6},{6,7},{8,9},{9,10},{10,11},{11... | collective-permute-start | bytes 1232 | tf_op jit(solution)/shard_map/ppermute | solution.py:23
  73.0 5.5 %collective-permute-start.11 = (f32[3,34,1]{2,1,0:T(8,128)S(1)}, f32[3,34,1]{2,1,0:T(8,128)S(1)}, u32[]{:S(2)}, u32[]{:S(2)}) collective-permute-start(f32[3,34,1]{2,1,0:T(8,128)S(1)} %get-tuple-element.69), channel_id=1, source_target_pairs={{1,0},{2,1},{3,2},{4,3},{5,4},{6,5},{7,6},{9,8},{10,9},{11,10},{12... | collective-permute-start | bytes 1232 | tf_op jit(solution)/shard_map/ppermute | solution.py:26
  78.9 5.4 %collective-permute-start.2 = (f32[4,130,1]{2,1,0:T(8,128)S(1)}, f32[4,130,1]{2,1,0:T(8,128)S(1)}, u32[]{:S(2)}, u32[]{:S(2)}) collective-permute-start(f32[4,130,1]{2,1,0:T(8,128)S(1)} %get-tuple-element.28), channel_id=1, source_target_pairs={{0,1},{1,2},{2,3},{3,4},{4,5},{5,6},{6,7},{8,9},{9,10},{10,11},{11... | collective-permute-start | bytes 6248 | tf_op jit(solution)/shard_map/ppermute | solution.py:23
  80.8 7.9 %collective-permute-start.3 = (f32[4,130,1]{2,1,0:T(8,128)S(1)}, f32[4,130,1]{2,1,0:T(8,128)S(1)}, u32[]{:S(2)}, u32[]{:S(2)}) collective-permute-start(f32[4,130,1]{2,1,0:T(8,128)S(1)} %get-tuple-element.29), channel_id=1, source_target_pairs={{1,0},{2,1},{3,2},{4,3},{5,4},{6,5},{7,6},{9,8},{10,9},{11,10},{12... | collective-permute-start | bytes 6248 | tf_op jit(solution)/shard_map/ppermute | solution.py:26
  89.4 0.9 copy-start.2
  90.5 5.9 %collective-permute-start.4 = (f32[4,1,256]{2,1,0:T(1,128)S(1)}, f32[4,1,256]{2,1,0:T(1,128)S(1)}, u32[]{:S(2)}, u32[]{:S(2)}) collective-permute-start(f32[4,1,256]{2,1,0:T(1,128)S(1)} %get-tuple-element.30), channel_id=1, source_target_pairs={{0,8},{8,16},{16,24},{1,9},{9,17},{17,25},{2,10},{10,18},{18,26},{... | collective-permute-start | bytes 12296 | tf_op jit(solution)/shard_map/ppermute | solution.py:23
  95.0 4.4 %collective-permute-start.5 = (f32[4,1,256]{2,1,0:T(1,128)S(1)}, f32[4,1,256]{2,1,0:T(1,128)S(1)}, u32[]{:S(2)}, u32[]{:S(2)}) collective-permute-start(f32[4,1,256]{2,1,0:T(1,128)S(1)} %get-tuple-element.31), channel_id=1, source_target_pairs={{8,0},{16,8},{24,16},{9,1},{17,9},{25,17},{10,2},{18,10},{26,18},{... | collective-permute-start | bytes 12296 | tf_op jit(solution)/shard_map/ppermute | solution.py:26
  99.6 29.0 %collective-permute-start.6 = (f32[4,130,1]{2,1,0:T(8,128)S(1)}, f32[4,130,1]{2,1,0:T(8,128)S(1)}, u32[]{:S(2)}, u32[]{:S(2)}) collective-permute-start(f32[4,130,1]{2,1,0:T(8,128)S(1)} %get-tuple-element.26), channel_id=1, source_target_pairs={{0,1},{1,2},{2,3},{3,4},{4,5},{5,6},{6,7},{8,9},{9,10},{10,11},{11... | collective-permute-start | bytes 6248 | tf_op jit(solution)/shard_map/ppermute | solution.py:23
  102.8 25.8 %collective-permute-start.7 = (f32[4,130,1]{2,1,0:T(8,128)S(1)}, f32[4,130,1]{2,1,0:T(8,128)S(1)}, u32[]{:S(2)}, u32[]{:S(2)}) collective-permute-start(f32[4,130,1]{2,1,0:T(8,128)S(1)} %get-tuple-element.27), channel_id=1, source_target_pairs={{1,0},{2,1},{3,2},{4,3},{5,4},{6,5},{7,6},{9,8},{10,9},{11,10},{12... | collective-permute-start | bytes 6248 | tf_op jit(solution)/shard_map/ppermute | solution.py:26
  129.7 0.7 copy-start.3
  154.3 0.6 copy-start.5
  155.0 97.6 %all-reduce.6.cloned.1.call-start = ((), (), s32[]{:S(2)}) async-start(), calls=%async_computation.1 | async-start | bytes 196608 | tf_op jit(solution)/shard_map/psum | solution.py:132
  253.5 4.4 %collective-permute-start.16 = (f32[3,1,256]{2,1,0:T(1,128)S(1)}, f32[3,1,256]{2,1,0:T(1,128)S(1)}, u32[]{:S(2)}, u32[]{:S(2)}) collective-permute-start(f32[3,1,256]{2,1,0:T(1,128)S(1)} %get-tuple-element.78), channel_id=1, source_target_pairs={{0,8},{8,16},{16,24},{1,9},{9,17},{17,25},{2,10},{10,18},{18,26},{... | collective-permute-start | bytes 9224 | tf_op jit(solution)/shard_map/ppermute | solution.py:23
  256.5 4.3 %collective-permute-start.17 = (f32[3,1,256]{2,1,0:T(1,128)S(1)}, f32[3,1,256]{2,1,0:T(1,128)S(1)}, u32[]{:S(2)}, u32[]{:S(2)}) collective-permute-start(f32[3,1,256]{2,1,0:T(1,128)S(1)} %get-tuple-element.79), channel_id=1, source_target_pairs={{8,0},{16,8},{24,16},{9,1},{17,9},{25,17},{10,2},{18,10},{26,18},{... | collective-permute-start | bytes 9224 | tf_op jit(solution)/shard_map/ppermute | solution.py:26
  261.0 7.5 %collective-permute-start.18 = (f32[3,34,1]{2,1,0:T(8,128)S(1)}, f32[3,34,1]{2,1,0:T(8,128)S(1)}, u32[]{:S(2)}, u32[]{:S(2)}) collective-permute-start(f32[3,34,1]{2,1,0:T(8,128)S(1)} %get-tuple-element.64), channel_id=1, source_target_pairs={{0,1},{1,2},{2,3},{3,4},{4,5},{5,6},{6,7},{8,9},{9,10},{10,11},{11... | collective-permute-start | bytes 1232 | tf_op jit(solution)/shard_map/ppermute | solution.py:23
  266.5 5.5 %collective-permute-start.19 = (f32[3,34,1]{2,1,0:T(8,128)S(1)}, f32[3,34,1]{2,1,0:T(8,128)S(1)}, u32[]{:S(2)}, u32[]{:S(2)}) collective-permute-start(f32[3,34,1]{2,1,0:T(8,128)S(1)} %get-tuple-element.65), channel_id=1, source_target_pairs={{1,0},{2,1},{3,2},{4,3},{5,4},{6,5},{7,6},{9,8},{10,9},{11,10},{12... | collective-permute-start | bytes 1232 | tf_op jit(solution)/shard_map/ppermute | solution.py:26
  273.5 5.2 %collective-permute-start.20 = (f32[3,1,256]{2,1,0:T(1,128)S(1)}, f32[3,1,256]{2,1,0:T(1,128)S(1)}, u32[]{:S(2)}, u32[]{:S(2)}) collective-permute-start(f32[3,1,256]{2,1,0:T(1,128)S(1)} %get-tuple-element.76), channel_id=1, source_target_pairs={{0,8},{8,16},{16,24},{1,9},{9,17},{17,25},{2,10},{10,18},{18,26},{... | collective-permute-start | bytes 9224 | tf_op jit(solution)/shard_map/ppermute | solution.py:23
  277.5 4.3 %collective-permute-start.21 = (f32[3,1,256]{2,1,0:T(1,128)S(1)}, f32[3,1,256]{2,1,0:T(1,128)S(1)}, u32[]{:S(2)}, u32[]{:S(2)}) collective-permute-start(f32[3,1,256]{2,1,0:T(1,128)S(1)} %get-tuple-element.77), channel_id=1, source_target_pairs={{8,0},{16,8},{24,16},{9,1},{17,9},{25,17},{10,2},{18,10},{26,18},{... | collective-permute-start | bytes 9224 | tf_op jit(solution)/shard_map/ppermute | solution.py:26
  281.9 5.2 %collective-permute-start.22 = (f32[3,34,1]{2,1,0:T(8,128)S(1)}, f32[3,34,1]{2,1,0:T(8,128)S(1)}, u32[]{:S(2)}, u32[]{:S(2)}) collective-permute-start(f32[3,34,1]{2,1,0:T(8,128)S(1)} %get-tuple-element.62), channel_id=1, source_target_pairs={{0,1},{1,2},{2,3},{3,4},{4,5},{5,6},{6,7},{8,9},{9,10},{10,11},{11... | collective-permute-start | bytes 1232 | tf_op jit(solution)/shard_map/ppermute | solution.py:23
  285.2 5.5 %collective-permute-start.23 = (f32[3,34,1]{2,1,0:T(8,128)S(1)}, f32[3,34,1]{2,1,0:T(8,128)S(1)}, u32[]{:S(2)}, u32[]{:S(2)}) collective-permute-start(f32[3,34,1]{2,1,0:T(8,128)S(1)} %get-tuple-element.63), channel_id=1, source_target_pairs={{1,0},{2,1},{3,2},{4,3},{5,4},{6,5},{7,6},{9,8},{10,9},{11,10},{12... | collective-permute-start | bytes 1232 | tf_op jit(solution)/shard_map/ppermute | solution.py:26
  292.2 3.9 %collective-permute-start.24 = (f32[3,1,256]{2,1,0:T(1,128)S(1)}, f32[3,1,256]{2,1,0:T(1,128)S(1)}, u32[]{:S(2)}, u32[]{:S(2)}) collective-permute-start(f32[3,1,256]{2,1,0:T(1,128)S(1)} %get-tuple-element.74), channel_id=1, source_target_pairs={{0,8},{8,16},{16,24},{1,9},{9,17},{17,25},{2,10},{10,18},{18,26},{... | collective-permute-start | bytes 9224 | tf_op jit(solution)/shard_map/ppermute | solution.py:23
  294.7 4.3 %collective-permute-start.25 = (f32[3,1,256]{2,1,0:T(1,128)S(1)}, f32[3,1,256]{2,1,0:T(1,128)S(1)}, u32[]{:S(2)}, u32[]{:S(2)}) collective-permute-start(f32[3,1,256]{2,1,0:T(1,128)S(1)} %get-tuple-element.75), channel_id=1, source_target_pairs={{8,0},{16,8},{24,16},{9,1},{17,9},{25,17},{10,2},{18,10},{26,18},{... | collective-permute-start | bytes 9224 | tf_op jit(solution)/shard_map/ppermute | solution.py:26
  299.2 5.2 %collective-permute-start.26 = (f32[3,34,1]{2,1,0:T(8,128)S(1)}, f32[3,34,1]{2,1,0:T(8,128)S(1)}, u32[]{:S(2)}, u32[]{:S(2)}) collective-permute-start(f32[3,34,1]{2,1,0:T(8,128)S(1)} %get-tuple-element.60), channel_id=1, source_target_pairs={{0,1},{1,2},{2,3},{3,4},{4,5},{5,6},{6,7},{8,9},{9,10},{10,11},{11... | collective-permute-start | bytes 1232 | tf_op jit(solution)/shard_map/ppermute | solution.py:23
  302.5 5.5 %collective-permute-start.27 = (f32[3,34,1]{2,1,0:T(8,128)S(1)}, f32[3,34,1]{2,1,0:T(8,128)S(1)}, u32[]{:S(2)}, u32[]{:S(2)}) collective-permute-start(f32[3,34,1]{2,1,0:T(8,128)S(1)} %get-tuple-element.61), channel_id=1, source_target_pairs={{1,0},{2,1},{3,2},{4,3},{5,4},{6,5},{7,6},{9,8},{10,9},{11,10},{12... | collective-permute-start | bytes 1232 | tf_op jit(solution)/shard_map/ppermute | solution.py:26
  309.5 3.9 %collective-permute-start.28 = (f32[3,1,256]{2,1,0:T(1,128)S(1)}, f32[3,1,256]{2,1,0:T(1,128)S(1)}, u32[]{:S(2)}, u32[]{:S(2)}) collective-permute-start(f32[3,1,256]{2,1,0:T(1,128)S(1)} %get-tuple-element.72), channel_id=1, source_target_pairs={{0,8},{8,16},{16,24},{1,9},{9,17},{17,25},{2,10},{10,18},{18,26},{... | collective-permute-start | bytes 9224 | tf_op jit(solution)/shard_map/ppermute | solution.py:23
  312.0 4.3 %collective-permute-start.29 = (f32[3,1,256]{2,1,0:T(1,128)S(1)}, f32[3,1,256]{2,1,0:T(1,128)S(1)}, u32[]{:S(2)}, u32[]{:S(2)}) collective-permute-start(f32[3,1,256]{2,1,0:T(1,128)S(1)} %get-tuple-element.73), channel_id=1, source_target_pairs={{8,0},{16,8},{24,16},{9,1},{17,9},{25,17},{10,2},{18,10},{26,18},{... | collective-permute-start | bytes 9224 | tf_op jit(solution)/shard_map/ppermute | solution.py:26
  316.4 5.2 %collective-permute-start.30 = (f32[3,34,1]{2,1,0:T(8,128)S(1)}, f32[3,34,1]{2,1,0:T(8,128)S(1)}, u32[]{:S(2)}, u32[]{:S(2)}) collective-permute-start(f32[3,34,1]{2,1,0:T(8,128)S(1)} %get-tuple-element.58), channel_id=1, source_target_pairs={{0,1},{1,2},{2,3},{3,4},{4,5},{5,6},{6,7},{8,9},{9,10},{10,11},{11... | collective-permute-start | bytes 1232 | tf_op jit(solution)/shard_map/ppermute | solution.py:23
  319.8 5.5 %collective-permute-start.31 = (f32[3,34,1]{2,1,0:T(8,128)S(1)}, f32[3,34,1]{2,1,0:T(8,128)S(1)}, u32[]{:S(2)}, u32[]{:S(2)}) collective-permute-start(f32[3,34,1]{2,1,0:T(8,128)S(1)} %get-tuple-element.59), channel_id=1, source_target_pairs={{1,0},{2,1},{3,2},{4,3},{5,4},{6,5},{7,6},{9,8},{10,9},{11,10},{12... | collective-permute-start | bytes 1232 | tf_op jit(solution)/shard_map/ppermute | solution.py:26
  326.7 3.9 %collective-permute-start.32 = (f32[3,1,256]{2,1,0:T(1,128)S(1)}, f32[3,1,256]{2,1,0:T(1,128)S(1)}, u32[]{:S(2)}, u32[]{:S(2)}) collective-permute-start(f32[3,1,256]{2,1,0:T(1,128)S(1)} %get-tuple-element.70), channel_id=1, source_target_pairs={{0,8},{8,16},{16,24},{1,9},{9,17},{17,25},{2,10},{10,18},{18,26},{... | collective-permute-start | bytes 9224 | tf_op jit(solution)/shard_map/ppermute | solution.py:23
  329.3 4.3 %collective-permute-start.33 = (f32[3,1,256]{2,1,0:T(1,128)S(1)}, f32[3,1,256]{2,1,0:T(1,128)S(1)}, u32[]{:S(2)}, u32[]{:S(2)}) collective-permute-start(f32[3,1,256]{2,1,0:T(1,128)S(1)} %get-tuple-element.71), channel_id=1, source_target_pairs={{8,0},{16,8},{24,16},{9,1},{17,9},{25,17},{10,2},{18,10},{26,18},{... | collective-permute-start | bytes 9224 | tf_op jit(solution)/shard_map/ppermute | solution.py:26
  333.7 5.2 %collective-permute-start.34 = (f32[3,34,1]{2,1,0:T(8,128)S(1)}, f32[3,34,1]{2,1,0:T(8,128)S(1)}, u32[]{:S(2)}, u32[]{:S(2)}) collective-permute-start(f32[3,34,1]{2,1,0:T(8,128)S(1)} %get-tuple-element.56), channel_id=1, source_target_pairs={{0,1},{1,2},{2,3},{3,4},{4,5},{5,6},{6,7},{8,9},{9,10},{10,11},{11... | collective-permute-start | bytes 1232 | tf_op jit(solution)/shard_map/ppermute | solution.py:23
  337.0 5.5 %collective-permute-start.35 = (f32[3,34,1]{2,1,0:T(8,128)S(1)}, f32[3,34,1]{2,1,0:T(8,128)S(1)}, u32[]{:S(2)}, u32[]{:S(2)}) collective-permute-start(f32[3,34,1]{2,1,0:T(8,128)S(1)} %get-tuple-element.57), channel_id=1, source_target_pairs={{1,0},{2,1},{3,2},{4,3},{5,4},{6,5},{7,6},{9,8},{10,9},{11,10},{12... | collective-permute-start | bytes 1232 | tf_op jit(solution)/shard_map/ppermute | solution.py:26
Sparse Core Ops, SparseCore 0:
  155.1 50.5 all-reduce.3
  208.9 43.6 all-reduce.5
